TPU v7x, 32 devices: a whole 2x2x4 slice. The times are simulated.
32 devices in a mesh: dp: 8 (over z, x), head: 4 (over y, core).
Axes of the slice: x: 2, y: 2, z: 4, core: 2. Of those that a mesh axis runs over, the one named last changes fastest.
Arguments:
- tokens: bfloat16 [32768, 768], P(('dp', 'head')), may hold values from -6 to 6
- cotangent: bfloat16 [32768, 768], P(('dp', 'head')), may hold values from -6 to 6
- lengths: int32 [32, 8], P('dp'), may hold values from 1 to 512, 1024 in all within a row
- masters: float32 [12, 768, 768], P(None, ('dp', 'head')), may hold values from -1 to 1
- vectors: float32 [12, 768], P(None, ('dp', 'head')), may hold values from -1.5 to 1.5
- left_stats: float32 [12, 768, 768], P(None, ('dp', 'head')), may hold values from -62914.56 to 254174.822, as said below
- right_stats: float32 [12, 768, 768], P(None, ('dp', 'head')), may hold values from -62914.56 to 254174.822, as said below
- vector_second: float32 [12, 768], P(None, ('dp', 'head')), may hold values from 163.84 to 1310.72
Outputs:
- output: bfloat16 [32768, 768], P(('dp', 'head'))
- input_grad: float32 [32768, 768], P(('dp', 'head'))
- block_grads: float32 [12, 768, 768], P(None, ('dp', 'head'))
- left_new: float32 [12, 768, 768], P(None, ('dp', 'head'))
- right_new: float32 [12, 768, 768], P(None, ('dp', 'head'))
- masters_new: float32 [12, 768, 768], P(None, ('dp', 'head'))
- vector_grads: float32 [12, 768], P(None, ('dp', 'head'))
- second_new: float32 [12, 768], P(None, ('dp', 'head'))
- vectors_new: float32 [12, 768], P(None, ('dp', 'head'))
Inputs may be any that keep to these rules, and one draw needn't show every extreme that they name: Row r of lengths lists, in order, the lengths of the documents packed into row r of 1024 tokens; each row sums to 1024. Each block of left_stats is symmetric. Each block of right_stats is symmetric.
All inputs are finite; a program needn't handle non-finite values.
Results may differ from a plain program's by a relative error of at most 0.012.
The roundings to bfloat16 on the way count: a program that leaves them out, or rounds other values in their place, can miss the bound.
Values may be sent and summed in bfloat16 or wider, within the bound.
A program may use at most 256 MiB of HBM per device.

v0:
```python
from functools import partial

import jax
import jax.numpy as jnp
import numpy as np
from jax import lax
from jax.sharding import PartitionSpec as P

D = 768
HEADS = 12
HD = 64
FF = 3072
PACK = 1024
NEWTON = 8
NB = 12


NORM_EPS = 1e-06
ROOT_EPS = 1e-06
MASK_FILL = -1e30
BETA = 0.95
BETA_TWO = 0.99
RATE = 1.0
RATE_VEC = 0.05
PRECISE = lax.Precision.HIGHEST


def segment_ids(lengths):
    doc_ends = jnp.cumsum(lengths, axis=-1)
    places = jnp.arange(PACK, dtype=jnp.int32)
    return jnp.sum((places[None, :, None] >= doc_ends[:, None, :]).astype(jnp.int32), axis=-1)


def layer_norm(summed, gain_row, shift_row):
    centred = summed - jnp.mean(summed, axis=-1, keepdims=True)
    inv_std = lax.rsqrt(jnp.mean(centred * centred, axis=-1, keepdims=True) + NORM_EPS)
    normed = centred * inv_std
    return (normed * gain_row + shift_row, normed, inv_std)


def norm_back(grad_out, normed, inv_std, gain_row):
    scaled = grad_out * gain_row
    mean_one = jnp.mean(scaled, axis=-1, keepdims=True)
    mean_two = jnp.mean(scaled * normed, axis=-1, keepdims=True)
    grad_in = inv_std * (scaled - mean_one - normed * mean_two)
    return (grad_in, jnp.sum(grad_out * normed, axis=0), jnp.sum(grad_out, axis=0))


def masked_scores(queries, key_rows, segments):
    scores = jnp.einsum(
        "qhd,khd->hqk", queries, key_rows, preferred_element_type=jnp.float32
    ) * HD ** (-0.5)
    same_doc = segments[:, None] == segments[None, :]
    return (jnp.where(same_doc[None], scores, MASK_FILL), same_doc)


def attend_forward(carry, packed):
    qkv_row, segments = packed
    scores, same_doc = masked_scores(qkv_row[:, 0], qkv_row[:, 1], segments)
    row_max = jnp.max(scores, axis=-1, keepdims=True)
    exp_terms = jnp.exp(scores - row_max)
    row_total = jnp.sum(exp_terms, axis=-1, keepdims=True)
    soft_low = (exp_terms / row_total).astype(jnp.bfloat16)
    context = jnp.einsum(
        "hqk,khd->qhd", soft_low, qkv_row[:, 2], preferred_element_type=jnp.float32
    )
    return (carry, (context.astype(jnp.bfloat16), (row_max + jnp.log(row_total))[..., 0]))


def attend_backward(carry, packed):
    qkv_row, grad_context, log_total, segments = packed
    queries, key_rows, value_rows = (qkv_row[:, 0], qkv_row[:, 1], qkv_row[:, 2])
    scores, same_doc = masked_scores(queries, key_rows, segments)
    soft = jnp.where(same_doc[None], jnp.exp(scores - log_total[..., None]), 0.0)
    soft_low = soft.astype(jnp.bfloat16)
    grad_value = jnp.einsum(
        "hqk,qhd->khd", soft_low, grad_context, preferred_element_type=jnp.float32
    )
    grad_soft = jnp.einsum(
        "qhd,khd->hqk", grad_context, value_rows, preferred_element_type=jnp.float32
    )
    grad_scores = (soft * (grad_soft - jnp.sum(grad_soft * soft, axis=-1, keepdims=True))).astype(
        jnp.bfloat16
    )
    grad_query = jnp.einsum(
        "hqk,khd->qhd", grad_scores, key_rows, preferred_element_type=jnp.float32
    ) * HD ** (-0.5)
    grad_key = jnp.einsum(
        "hqk,qhd->khd", grad_scores, queries, preferred_element_type=jnp.float32
    ) * HD ** (-0.5)
    stacked = jnp.stack([grad_query, grad_key, grad_value], axis=1).astype(jnp.bfloat16)
    return (carry, stacked)


def batched(left, right):
    return jnp.einsum("kij,kjl->kil", left, right, precision=PRECISE)


def gather_iterate(matrix_rows):
    return lax.all_gather(matrix_rows, "head", axis=1, tiled=True)


def whole_root(matrix_rows):
    return lax.all_gather(matrix_rows, "head", axis=1, tiled=True)


def move_to_owners(grad_slots, stat_slots):
    return (
        lax.all_to_all(grad_slots, "dp", split_axis=1, concat_axis=1, tiled=True),
        lax.all_to_all(stat_slots, "dp", split_axis=1, concat_axis=1, tiled=True),
    )


def send_home(update_rows, stat_rows):
    return (
        lax.all_to_all(update_rows, "dp", split_axis=1, concat_axis=1, tiled=True),
        lax.all_to_all(stat_rows, "dp", split_axis=1, concat_axis=1, tiled=True),
    )


def inverse_root_rows(stat_rows, first_row):
    share = stat_rows.shape[1]
    identity = jnp.eye(D, dtype=jnp.float32)
    identity_rows = (
        lax.broadcasted_iota(jnp.int32, (share, D), 1)
        == lax.broadcasted_iota(jnp.int32, (share, D), 0) + first_row
    ).astype(jnp.float32)
    moving_rows = stat_rows
    inverse_rows = identity_rows
    for iteration in range(NEWTON):
        moving = gather_iterate(moving_rows)
        if iteration == 0:
            frob_norm = jnp.sqrt(jnp.sum(moving * moving, axis=(1, 2), keepdims=True) + ROOT_EPS)
            moving = moving / frob_norm
            moving_rows = moving_rows / frob_norm
            inverse_rows = lax.rsqrt(jnp.sqrt(frob_norm)) * identity_rows
        factor = (5.0 * identity - moving) * 0.25
        factor_rows = (5.0 * identity_rows - moving_rows) * 0.25
        inverse_rows = batched(inverse_rows, factor)
        if iteration + 1 < NEWTON:
            power_rows = batched(batched(batched(factor_rows, factor), factor), factor)
            moving_rows = batched(power_rows, moving)
    return inverse_rows


def to_owner_basis(matrix_rows, owner_count, head_count):
    leading = matrix_rows.shape[:2]
    pieces = matrix_rows.reshape(
        leading + (owner_count, head_count, D // (owner_count * head_count))
    )
    return jnp.swapaxes(pieces, 2, 3).reshape(leading + (D,))


def from_owner_basis(matrix_rows, owner_count, head_count):
    leading = matrix_rows.shape[:2]
    pieces = matrix_rows.reshape(
        leading + (head_count, owner_count, D // (owner_count * head_count))
    )
    return jnp.swapaxes(pieces, 2, 3).reshape(leading + (D,))


def to_slots(rest_rows, slot_total, owner_count):
    padded = jnp.pad(rest_rows, ((0, slot_total - rest_rows.shape[0]), (0, 0), (0, 0)))
    return padded.reshape(
        slot_total // owner_count, owner_count, rest_rows.shape[1], rest_rows.shape[2]
    )


def renew_roots(got_grad, got_stats, item_block, transposed, first_row, owner_count, head_count):
    share = got_grad.shape[1]
    grad_own = to_owner_basis(got_grad, owner_count, head_count)
    grad_whole = lax.all_gather(grad_own, "head", axis=1, tiled=True)
    chosen = grad_whole[item_block]
    flipped = jnp.where(transposed, jnp.swapaxes(chosen, 1, 2), chosen)
    own_rows = lax.dynamic_slice_in_dim(flipped, first_row, share, axis=1)
    stats_new = BETA * to_owner_basis(got_stats, owner_count, head_count) + (
        1.0 - BETA
    ) * jnp.einsum("kid,kjd->kij", own_rows, flipped, precision=PRECISE)
    roots = inverse_root_rows(stats_new, first_row)
    return (grad_whole, stats_new, roots)


def on_device(tokens, cotangent, lengths, masters, vectors, left_stats, right_stats, vector_second):
    head_count = lax.axis_size("head")
    owner_count = lax.axis_size("dp")
    token_count = tokens.shape[0]
    local_heads = HEADS // head_count
    head_width = D // head_count
    ffn_blocks = FF // D
    group_rows = head_count * token_count // PACK
    row_share = masters.shape[1]
    blocks, params = (
        lax.all_gather(masters.astype(jnp.bfloat16), ("dp", "head"), axis=1, tiled=True),
        lax.all_gather(vectors.astype(jnp.bfloat16), ("dp", "head"), axis=1, tiled=True),
    )
    params = params.astype(jnp.float32)
    qkv_weight = blocks[0:3].reshape(3, D, head_count, head_width)
    out_weight = blocks[3]
    up_weight = blocks[4 : 4 + ffn_blocks]
    down_weight = blocks[4 + ffn_blocks :]
    qkv_bias = jnp.stack([params[0], jnp.zeros_like(params[0]), params[1]]).reshape(
        3, head_count, head_width
    )
    gain_one, shift_one = (params[4 + ffn_blocks], params[5 + ffn_blocks])
    gain_two, shift_two = (params[6 + ffn_blocks], params[7 + ffn_blocks])
    projected = jnp.einsum(
        "td,cdnf->tncf", tokens, qkv_weight, preferred_element_type=jnp.float32
    ) + jnp.transpose(qkv_bias, (1, 0, 2))
    projected = projected.astype(jnp.bfloat16).reshape(token_count, head_count, 3 * head_width)
    by_head = lax.all_to_all(projected, "head", split_axis=1, concat_axis=0, tiled=True)
    by_head = by_head.reshape(group_rows, PACK, 3, local_heads, HD)
    segments = segment_ids(lengths)
    unused, (context, log_total) = lax.scan(attend_forward, 0, (by_head, segments))
    context = lax.all_to_all(
        context.reshape(group_rows * PACK, 1, head_width),
        "head",
        split_axis=0,
        concat_axis=1,
        tiled=True,
    )
    context = context.reshape(token_count, D)
    attn_out = jnp.dot(context, out_weight, preferred_element_type=jnp.float32) + params[2]
    hidden, normed_one, inv_one = layer_norm(
        tokens.astype(jnp.float32) + attn_out, gain_one, shift_one
    )
    hidden_low = hidden.astype(jnp.bfloat16)
    inner_act = (
        jnp.einsum("td,cdf->tcf", hidden_low, up_weight, preferred_element_type=jnp.float32)
        + params[3 : 3 + ffn_blocks]
    )
    activation, gelu_back = jax.vjp(partial(jax.nn.gelu, approximate=False), inner_act)
    act_low = activation.astype(jnp.bfloat16)
    ffn_out = (
        jnp.einsum("tcf,cfd->td", act_low, down_weight, preferred_element_type=jnp.float32)
        + params[3 + ffn_blocks]
    )
    output, normed_two, inv_two = layer_norm(hidden + ffn_out, gain_two, shift_two)
    grad_sum_two, grad_gain_two, grad_shift_two = norm_back(
        cotangent.astype(jnp.float32), normed_two, inv_two, gain_two
    )
    grad_ffn = grad_sum_two.astype(jnp.bfloat16)
    grad_down = jnp.einsum("tcf,td->cfd", act_low, grad_ffn, preferred_element_type=jnp.float32)
    grad_act = jnp.einsum("td,cfd->tcf", grad_ffn, down_weight, preferred_element_type=jnp.float32)
    grad_inner = gelu_back(grad_act)[0].astype(jnp.bfloat16)
    grad_up = jnp.einsum("td,tcf->cdf", hidden_low, grad_inner, preferred_element_type=jnp.float32)
    grad_hidden = grad_sum_two + jnp.einsum(
        "tcf,cdf->td", grad_inner, up_weight, preferred_element_type=jnp.float32
    )
    grad_sum_one, grad_gain_one, grad_shift_one = norm_back(
        grad_hidden, normed_one, inv_one, gain_one
    )
    grad_attn = grad_sum_one.astype(jnp.bfloat16)
    grad_out_weight = jnp.einsum(
        "td,te->de", context, grad_attn, preferred_element_type=jnp.float32
    )
    grad_context = jnp.einsum(
        "te,de->td", grad_attn, out_weight, preferred_element_type=jnp.float32
    ).astype(jnp.bfloat16)
    grad_context = lax.all_to_all(
        grad_context.reshape(token_count, head_count, head_width),
        "head",
        split_axis=1,
        concat_axis=0,
        tiled=True,
    )
    grad_context = grad_context.reshape(group_rows, PACK, local_heads, HD)
    unused, grad_heads = lax.scan(attend_backward, 0, (by_head, grad_context, log_total, segments))
    grad_heads = lax.all_to_all(
        grad_heads.reshape(group_rows * PACK, 1, 3 * head_width),
        "head",
        split_axis=0,
        concat_axis=1,
        tiled=True,
    )
    grad_qkv = grad_heads.reshape(token_count, head_count, 3, head_width)
    grad_qkv_weight = jnp.einsum(
        "td,tncf->cdnf", tokens, grad_qkv, preferred_element_type=jnp.float32
    ).reshape(3, D, D)
    input_grad = grad_sum_one + jnp.einsum(
        "tncf,cdnf->td", grad_qkv, qkv_weight, preferred_element_type=jnp.float32
    )
    bias_sums = jnp.sum(grad_qkv, axis=0, dtype=jnp.float32)
    terms = jnp.concatenate([grad_qkv_weight, grad_out_weight[None], grad_up, grad_down], axis=0)
    vec_terms = jnp.concatenate(
        [
            jnp.stack(
                [
                    bias_sums[:, 0].reshape(D),
                    bias_sums[:, 2].reshape(D),
                    jnp.sum(grad_attn, axis=0, dtype=jnp.float32),
                ]
            ),
            jnp.sum(grad_inner, axis=0, dtype=jnp.float32),
            jnp.stack(
                [
                    jnp.sum(grad_ffn, axis=0, dtype=jnp.float32),
                    grad_gain_one,
                    grad_shift_one,
                    grad_gain_two,
                    grad_shift_two,
                ]
            ),
        ],
        axis=0,
    )
    grad_rest, vec_grad = (
        lax.psum_scatter(terms, ("dp", "head"), scatter_dimension=1, tiled=True),
        lax.psum_scatter(vec_terms, ("dp", "head"), scatter_dimension=1, tiled=True),
    )
    share = D // head_count
    first_row = lax.axis_index("head") * share

    def back_rows(matrix_rows):
        return from_owner_basis(matrix_rows, owner_count, head_count).reshape(
            matrix_rows.shape[0], owner_count, row_share, D
        )

    def at_rest(slotted_rows, count):
        return slotted_rows.reshape(-1, row_share, D)[:count]

    slot_depth = (NB + owner_count - 1) // owner_count
    slot_total = slot_depth * owner_count
    stat_slots = jnp.concatenate(
        [
            to_slots(left_stats, slot_total, owner_count),
            to_slots(right_stats, slot_total, owner_count),
        ],
        axis=0,
    )
    got_grad, got_stats = move_to_owners(to_slots(grad_rest, slot_total, owner_count), stat_slots)
    item_block = np.concatenate([np.arange(slot_depth), np.arange(slot_depth)])
    transposed = jnp.asarray(
        np.concatenate([np.zeros(slot_depth, bool), np.ones(slot_depth, bool)])
    )[:, None, None]
    grad_whole, stats_new, roots = renew_roots(
        got_grad.reshape(slot_depth, share, D),
        got_stats.reshape(2 * slot_depth, share, D),
        item_block,
        transposed,
        first_row,
        owner_count,
        head_count,
    )
    right_whole = whole_root(roots[slot_depth:])
    update = batched(batched(roots[:slot_depth], grad_whole), right_whole)
    update_back, stats_back = send_home(back_rows(update), back_rows(stats_new))
    update_rest = at_rest(update_back, NB)
    left_new = at_rest(stats_back[:slot_depth], NB)
    right_new = at_rest(stats_back[slot_depth:], NB)
    masters_new = masters - RATE * update_rest
    second_new = BETA_TWO * vector_second + (1.0 - BETA_TWO) * vec_grad * vec_grad
    vectors_new = vectors - RATE_VEC * vec_grad / (jnp.sqrt(second_new) + 1e-08)
    return (
        output.astype(jnp.bfloat16),
        input_grad,
        grad_rest,
        left_new,
        right_new,
        masters_new,
        vec_grad,
        second_new,
        vectors_new,
    )


def solution(mesh):
    placed = (
        P(("dp", "head"), None),
        P(("dp", "head"), None),
        P("dp", None),
        P(None, ("dp", "head"), None),
        P(None, ("dp", "head")),
        P(None, ("dp", "head"), None),
        P(None, ("dp", "head"), None),
        P(None, ("dp", "head")),
    )
    return jax.shard_map(
        on_device,
        mesh=mesh,
        in_specs=placed,
        out_specs=(
            P(("dp", "head"), None),
            P(("dp", "head"), None),
            P(None, ("dp", "head"), None),
            P(None, ("dp", "head"), None),
            P(None, ("dp", "head"), None),
            P(None, ("dp", "head"), None),
            P(None, ("dp", "head")),
            P(None, ("dp", "head")),
            P(None, ("dp", "head")),
        ),
        check_vma=False,
    )
```

profile of v0, /device:TPU:11, one launch (start us, length us, event | category | flops | bytes accessed | tf_op | source)
XLA Modules:
  0.0 2201.2 jit_solution(1997860088552993910)
XLA Ops:
  9.9 32.7 %all-gather = bf16[32,24,12]{1,2,0:T(8,128)(2,1)S(1)} all-gather(bf16[1,24,12]{1,2,0:T(8,128)(2,1)S(1)} %convert_bitcast_fusion), channel_id=1, replica_groups=mesh['dp'=8,'head'=4] {'dp','head'}, dimensions={0}, use_global_device_ids=true | all-gather | bytes 19008 | tf_op jit(solution)/shard_map/all_gather | solution.py:194
  43.9 71.6 %all-gather.13.cloned.1.call-done = bf16[12,768,768]{2,1,0:T(8,128)(2,1)} async-done(((bf16[12,24,768]{2,1,0:T(8,128)(2,1)}), bf16[12,768,768]{2,1,0:T(8,128)(2,1)}) %all-gather.13.cloned.1.call-update) | async-done | bytes 14155792 | tf_op jit(solution)/shard_map/all_gather | solution.py:193
  136.0 52.7 %all-to-all-done = bf16[1024,4,576]{0,2,1:T(8,128)(2,1)} async-done(((bf16[1024,4,576]{0,2,1:T(8,128)(2,1)}), bf16[1024,4,576]{0,2,1:T(8,128)(2,1)}, u32[]{:S(2)}, u32[]{:S(2)}) %all-to-all-start) | async-done | bytes 4718624 | tf_op jit(solution)/shard_map/all_to_all | solution.py:210
  188.7 58.7 %while.22 = (s32[]{:T(128)}, bf16[4,1024,3,64]{1,3,2,0:T(8,128)(2,1)}, f32[4,3,1024]{2,1,0:T(4,128)S(1)}, bf16[4,1024,3,3,64]{1,4,3,2,0:T(8,128)(2,1)}, s32[4,1024]{1,0:T(4,128)S(1)}, /*index=5*/s32[]{:T(128)}) while((s32[]{:T(128)}, bf16[4,1024,3,64]{1,3,2,0:T(8,128)(2,1)}, f32[4,3,1024]{2,1,0:T(4,128)S(1)}, ...), condition=%wide.region_5.6_spmd, body=%wide.region_2.5_spmd.sunk | while | flops 844297216 | bytes 54911124 | solution.py:213
  322.2 32.2 %multiply_convert_fusion.1 = (bf16[1024,4,768]{2,0,1:T(8,128)(2,1)}, f32[1024,4,768]{2,0,1:T(8,128)}) fusion(f32[1024,4,768]{2,0,1:T(8,128)} %get-tuple-element.197, f32[4,768]{1,0:T(4,128)S(1)} %slice.122, u8[1024,768]{1,0:T(8,128)(4,1)S(1)} %get-tuple-element.136, u8[1024,768]{1,0:T(8,128)(4,1)S(1)} %get-tuple-element.135), kind=kLoop, calls=%fused_computation.58 | loop fusion | flops 223346688 | bytes 33042432 | tf_op jit(solution)/shard_map/convert_element_type | solution.py:232
  370.0 18.1 convert_reduce_fusion
  410.7 19.2 all-to-all-done.2
  429.9 90.2 %while.23 = (s32[]{:T(128)}, bf16[4,1024,3,3,64]{1,4,3,2,0:T(8,128)(2,1)}, bf16[4,1024,3,3,64]{1,4,3,2,0:T(8,128)(2,1)}, s32[4,1024]{1,0:T(4,128)S(1)}, f32[4,3,...) while((s32[]{:T(128)}, bf16[4,1024,3,3,64]{1,4,3,2,0:T(8,128)(2,1)}, ...), condition=%wide.region_16.17_spmd, body=%wide.region_14.16_spmd.sunk | while | flops 2050290688 | bytes 130363536 | solution.py:267
  590.0 29.6 %all-to-all-done.3 = bf16[4,2,294912]{2,1,0:T(2,128)(2,1)} async-done(((bf16[4,2,294912]{2,1,0:T(2,128)(2,1)}), bf16[4,2,294912]{2,1,0:T(2,128)(2,1)}, u32[]{:S(2)}, u32[]{:S(2)}) %all-to-all-start.3) | async-done | bytes 4718624 | tf_op jit(solution)/shard_map/all_to_all | solution.py:268
  658.7 19.8 pad_maximum_fusion
  678.5 33.6 %copy.306 = f32[12,768,768]{2,0,1:T(8,128)} copy(f32[12,768,768]{1,2,0:T(8,128)} %pad_maximum_fusion) | data formatting | bytes 56623104 | tf_op jit(solution)/shard_map/concatenate | solution.py:283
  712.2 347.2 %reduce-scatter.3.cloned.1.call-done = f32[12,24,768]{2,0,1:T(8,128)} async-done(((f32[12,768,768]{2,0,1:T(8,128)}), f32[12,24,768]{2,0,1:T(8,128)}) %reduce-scatter.3.cloned.1.call-update) | async-done | bytes 884752 | tf_op jit(solution)/shard_map/reduce_scatter | solution.py:307
  1061.4 30.8 %all_to_all.80 = f32[2,8,24,768]{3,2,0,1:T(8,128)S(1)} all-to-all(f32[2,8,24,768]{3,2,0,1:T(8,128)S(1)} %copy.310), channel_id=1, replica_groups=mesh['dp'=8,'head'=4] {'dp'}, dimensions={1} | all-to-all | bytes 2359296 | tf_op jit(solution)/shard_map/all_to_all | solution.py:109
  1117.3 51.3 %all-to-all-done.4 = f32[4,8,24,768]{3,2,0,1:T(8,128)S(1)} async-done(((f32[4,8,24,768]{3,2,0,1:T(8,128)}), f32[4,8,24,768]{3,2,0,1:T(8,128)S(1)}, u32[]{:S(2)}, u32[]{:S(2)}) %all-to-all-start.4) | async-done | bytes 2359328 | tf_op jit(solution)/shard_map/all_to_all | solution.py:110
  1169.0 18.4 mul.321
  1245.3 65.7 %all-gather.17.cloned.1.call-done = f32[4,768,768]{2,1,0:T(8,128)} async-done(((f32[4,192,768]{2,1,0:T(8,128)}), f32[4,768,768]{2,1,0:T(8,128)}) %all-gather.17.cloned.1.call-update) | async-done | bytes 9437200 | tf_op jit(solution)/shard_map/all_gather | solution.py:100
  1351.4 64.4 %all-gather.19.cloned.1.call-done = f32[4,768,768]{2,1,0:T(8,128)} async-done(((f32[4,192,768]{2,1,0:T(8,128)}), f32[4,768,768]{2,1,0:T(8,128)}) %all-gather.19.cloned.1.call-update) | async-done | bytes 9437200 | tf_op jit(solution)/shard_map/all_gather | solution.py:100
  1450.6 64.4 %all-gather.21.cloned.1.call-done = f32[4,768,768]{2,1,0:T(8,128)} async-done(((f32[4,192,768]{2,1,0:T(8,128)}), f32[4,768,768]{2,1,0:T(8,128)}) %all-gather.21.cloned.1.call-update) | async-done | bytes 9437200 | tf_op jit(solution)/shard_map/all_gather | solution.py:100
  1549.8 64.3 %all-gather.23.cloned.1.call-done = f32[4,768,768]{2,1,0:T(8,128)} async-done(((f32[4,192,768]{2,1,0:T(8,128)}), f32[4,768,768]{2,1,0:T(8,128)}) %all-gather.23.cloned.1.call-update) | async-done | bytes 9437200 | tf_op jit(solution)/shard_map/all_gather | solution.py:100
  1648.9 64.4 %all-gather.25.cloned.1.call-done = f32[4,768,768]{2,1,0:T(8,128)} async-done(((f32[4,192,768]{2,1,0:T(8,128)}), f32[4,768,768]{2,1,0:T(8,128)}) %all-gather.25.cloned.1.call-update) | async-done | bytes 9437200 | tf_op jit(solution)/shard_map/all_gather | solution.py:100
  1748.2 64.4 %all-gather.27.cloned.1.call-done = f32[4,768,768]{2,1,0:T(8,128)} async-done(((f32[4,192,768]{2,1,0:T(8,128)}), f32[4,768,768]{2,1,0:T(8,128)}) %all-gather.27.cloned.1.call-update) | async-done | bytes 9437200 | tf_op jit(solution)/shard_map/all_gather | solution.py:100
  1847.4 64.4 %all-gather.29.cloned.1.call-done = f32[4,768,768]{2,1,0:T(8,128)} async-done(((f32[4,192,768]{2,1,0:T(8,128)}), f32[4,768,768]{2,1,0:T(8,128)}) %all-gather.29.cloned.1.call-update) | async-done | bytes 9437200 | tf_op jit(solution)/shard_map/all_gather | solution.py:100
  2104.4 17.2 all-to-all-done.6
  2146.6 40.1 %all-reduce.3 = f32[12,768]{1,0:T(8,128)S(1)} all-reduce(f32[12,768]{1,0:T(8,128)S(1)} %concatenate.19), channel_id=3, replica_groups=mesh['dp'=8,'head'=4] {'dp','head'}, use_global_device_ids=true, to_apply=%region_27.28.clone | all-reduce | flops 9216 | bytes 73728
  (449 shorter events, 918.4 us)
Async XLA Ops:
  7.2 108.3 %all-gather.13.cloned.1.call-start = ((), (), s32[]{:S(2)}) async-start(), calls=%async_computation.9 | async-start | bytes 14598144 | tf_op jit(solution)/shard_map/all_gather | solution.py:193
  130.2 58.4 %all-to-all-start = ((bf16[1024,4,576]{0,2,1:T(8,128)(2,1)}), bf16[1024,4,576]{0,2,1:T(8,128)(2,1)}, u32[]{:S(2)}, u32[]{:S(2)}) async-start(bf16[1024,4,576]{0,2,1:T(8,128)(2,1)} %bitcast.279), calls=%async_computation | async-start | bytes 9437184 | tf_op jit(solution)/shard_map/all_to_all | solution.py:210
  260.8 23.9 %all-to-all-start.1 = ((bf16[4,2,98304]{2,1,0:T(2,128)(2,1)}), bf16[4,2,98304]{2,1,0:T(2,128)(2,1)S(1)}, u32[]{:S(2)}, u32[]{:S(2)}) async-start(bf16[4,2,98304]{2,1,0:T(2,128)(2,1)} %reshape.369), calls=%async_computation.1 | async-start | bytes 3145728 | tf_op jit(solution)/shard_map/all_to_all | solution.py:214
  305.7 94.0 %copy-start.32 = (f32[1024]{0:T(1024)}, f32[1024]{0:T(1024)S(1)}, u32[]{:S(2)}) copy-start(f32[1024]{0:T(1024)S(1)} %broadcast_multiply_fusion.6) | copy-start | bytes 12292
  306.1 93.6 %copy-start.41 = (f32[1024]{0:T(1024)}, f32[1024]{0:T(1024)S(1)}, u32[]{:S(2)}) copy-start(f32[1024]{0:T(1024)S(1)} %add_rsqrt_fusion.1) | copy-start | bytes 12292
  306.4 48.0 %slice-start.9 = ((s8[14155776]{0:T(1024)(128)(4,1)}), s8[1572864]{0:T(1024)(128)(4,1)S(1)}, s32[]{:S(2)}) async-start(s8[14155776]{0:T(1024)(128)(4,1)} %bitcast.280), calls=%async_computation.30 | async-start | bytes 3145728
  306.4 48.0 %slice-start.10 = ((s8[14155776]{0:T(1024)(128)(4,1)}), s8[4194304]{0:T(1024)(128)(4,1)S(1)}, s32[]{:S(2)}) async-start(s8[14155776]{0:T(1024)(128)(4,1)} %bitcast.280), calls=%async_computation.31 | async-start | bytes 8388608
  306.4 48.0 %slice-start.11 = ((s8[14155776]{0:T(1024)(128)(4,1)}), s8[4194304]{0:T(1024)(128)(4,1)S(1)}, s32[]{:S(2)}) async-start(s8[14155776]{0:T(1024)(128)(4,1)} %bitcast.280), calls=%async_computation.32 | async-start | bytes 8388608
  406.1 23.8 %all-to-all-start.2 = ((bf16[1024,4,192]{0,2,1:T(8,128)(2,1)}), bf16[1024,4,192]{0,2,1:T(8,128)(2,1)S(1)}, u32[]{:S(2)}, u32[]{:S(2)}) async-start(bf16[1024,4,192]{0,2,1:T(8,128)(2,1)} %bitcast.300), calls=%async_computation.2 | async-start | bytes 3145728 | tf_op jit(solution)/shard_map/all_to_all | solution.py:259
  560.5 59.1 %all-to-all-start.3 = ((bf16[4,2,294912]{2,1,0:T(2,128)(2,1)}), bf16[4,2,294912]{2,1,0:T(2,128)(2,1)}, u32[]{:S(2)}, u32[]{:S(2)}) async-start(bf16[4,2,294912]{2,1,0:T(2,128)(2,1)} %reshape.371), calls=%async_computation.3 | async-start | bytes 9437184 | tf_op jit(solution)/shard_map/all_to_all | solution.py:268
  566.6 492.8 %reduce-scatter.3.cloned.1.call-start = ((), (), s32[]{:S(2)}) async-start(), calls=%async_computation.10 | async-start | bytes 38928384 | tf_op jit(solution)/shard_map/reduce_scatter | solution.py:307
  712.1 488.7 %all-gather.15.cloned.1.call-start = ((), (), s32[]{:S(2)}) async-start(), calls=%async_computation.11 | async-start | bytes 5898240 | tf_op jit(solution)/shard_map/all_gather | solution.py:172
  1111.3 57.3 %all-to-all-start.4 = ((f32[4,8,24,768]{3,2,0,1:T(8,128)}), f32[4,8,24,768]{3,2,0,1:T(8,128)S(1)}, u32[]{:S(2)}, u32[]{:S(2)}) async-start(f32[4,8,24,768]{3,2,0,1:T(8,128)} %copy.307), calls=%async_computation.5 | async-start | bytes 4718592 | tf_op jit(solution)/shard_map/all_to_all | solution.py:110
  1117.3 193.7 %all-gather.17.cloned.1.call-start = ((), (), s32[]{:S(2)}) async-start(), calls=%async_computation.12 | async-start | bytes 11796480 | tf_op jit(solution)/shard_map/all_gather | solution.py:100
  1244.5 171.2 %all-gather.19.cloned.1.call-start = ((), (), s32[]{:S(2)}) async-start(), calls=%async_computation.13 | async-start | bytes 11796480 | tf_op jit(solution)/shard_map/all_gather | solution.py:100
  1351.3 163.6 %all-gather.21.cloned.1.call-start = ((), (), s32[]{:S(2)}) async-start(), calls=%async_computation.14 | async-start | bytes 11796480 | tf_op jit(solution)/shard_map/all_gather | solution.py:100
  1450.5 163.6 %all-gather.23.cloned.1.call-start = ((), (), s32[]{:S(2)}) async-start(), calls=%async_computation.15 | async-start | bytes 11796480 | tf_op jit(solution)/shard_map/all_gather | solution.py:100
  1549.7 163.6 %all-gather.25.cloned.1.call-start = ((), (), s32[]{:S(2)}) async-start(), calls=%async_computation.16 | async-start | bytes 11796480 | tf_op jit(solution)/shard_map/all_gather | solution.py:100
  1648.9 163.6 %all-gather.27.cloned.1.call-start = ((), (), s32[]{:S(2)}) async-start(), calls=%async_computation.17 | async-start | bytes 11796480 | tf_op jit(solution)/shard_map/all_gather | solution.py:100
  1748.1 163.6 %all-gather.29.cloned.1.call-start = ((), (), s32[]{:S(2)}) async-start(), calls=%async_computation.18 | async-start | bytes 11796480 | tf_op jit(solution)/shard_map/all_gather | solution.py:100
  1847.3 171.1 %all-gather.31.cloned.1.call-start = ((), (), s32[]{:S(2)}) async-start(), calls=%async_computation.19 | async-start | bytes 11796480 | tf_op jit(solution)/shard_map/all_gather | solution.py:100
  1946.3 134.2 %all-gather.33.cloned.1.call-start = ((), (), s32[]{:S(2)}) async-start(), calls=%async_computation.20 | async-start | bytes 5898240 | tf_op jit(solution)/shard_map/all_gather | solution.py:104
  2064.5 57.1 %all-to-all-start.6 = ((f32[4,8,24,768]{3,2,0,1:T(8,128)}), f32[4,8,24,768]{3,2,0,1:T(8,128)}, u32[]{:S(2)}, u32[]{:S(2)}) async-start(f32[4,8,24,768]{3,2,0,1:T(8,128)} %copy.318), calls=%async_computation.7 | async-start | bytes 4718592 | tf_op jit(solution)/shard_map/all_to_all | solution.py:117
  2121.6 71.2 %all-to-all-start.7 = ((f32[2,8,24,768]{3,2,0,1:T(8,128)}), f32[2,8,24,768]{3,2,0,1:T(8,128)S(1)}, u32[]{:S(2)}, u32[]{:S(2)}) async-start(f32[2,8,24,768]{3,2,0,1:T(8,128)} %copy.323), calls=%async_computation.8 | async-start | bytes 2359296 | tf_op jit(solution)/shard_map/all_to_all | solution.py:116
  (84 other events, 826.2 us)
Sparse Core Ops, SparseCore 0:
  11.4 103.9 all-gather.12
  712.3 347.0 reduce-scatter.2
  1109.4 39.3 all-gather.14
  1244.7 66.2 all-gather.16
  1351.5 64.2 all-gather.18
  1450.7 64.2 all-gather.20
  1549.8 64.2 all-gather.22
  1649.0 64.2 all-gather.24
  1748.2 64.2 all-gather.26
  1847.5 64.2 all-gather.28
  1946.4 64.2 all-gather.30
  2032.2 37.4 all-gather.32
where the time goes:
time: 2210 us; the launch traced here: 2200 us
  waiting for transfers between devices  1060 us (48%)
  matrix products  552 us (25%)
  local copies, waits for them, and re-layouts  290 us (13%)
  other arithmetic  143 us (6%)
  blocking collectives  104 us (5%)
  starting transfers between devices  39.7 us (2%)
    all_gather x8, waiting for transfers between devices, gather_iterate(): return lax.all_gather(matrix_rows, 'head', axis=1, tiled=True)  452 us
    reduce_scatter x1, waiting for transfers between devices, on_device(): lax.psum_scatter(terms, ('dp', 'head'), scatter_dimension=1, tiled=True)  347 us
    dot_general x38, matrix products, batched(): return jnp.einsum('kij,kjl->kil', left, right, precision=PRECISE)  342 us
    all_gather x1, waiting for transfers between devices, on_device(): lax.all_gather(masters.astype(jnp.bfloat16), ('dp', 'head'), axis=1, tile...  71.6 us
    unnamed x168, local copies, waits for them, and re-layouts  60.7 us
    all_to_all x1, waiting for transfers between devices, on_device(): lax.all_to_all(projected, 'head', split_axis=1, concat_axis=0, tiled=True)  52.7 us
    all_to_all x1, waiting for transfers between devices, move_to_owners(): lax.all_to_all(stat_slots, 'dp', split_axis=1, concat_axis=1, tiled=True)  51.3 us
  transfers between devices with their start and end apart: 19, of which 15 were waited for; matrix products, arithmetic and copies ran while one was open for 10% of the time, Pallas kernels for 0%

commit v1 on v0

v1 whole, which is shorter than its diff:
```python
import jax, jax.numpy as jnp, numpy as np
from functools import partial
from jax import lax
from jax.experimental import pallas as pl
from jax.experimental.pallas import tpu as pltpu
from jax.sharding import PartitionSpec as P

D=768; HEADS=12; HD=64; FF=3072; PACK=1024; NEWTON=8; NB=12
NORM_EPS=1e-6
f32=jnp.float32; bf16=jnp.bfloat16
BIG=1e30
QB=256
def dot(a,b,ca=1,cb=0):
    return lax.dot_general(a,b,(((ca,),(cb,)),((),())),preferred_element_type=f32)

def doc_column(len_ref, shape, dim):
    t=lax.broadcasted_iota(jnp.int32,shape,dim)
    end=jnp.int32(0); doc=jnp.zeros(shape,jnp.int32)
    for j in range(8):
        end=end+len_ref[0,j]
        doc=doc+(t>=end).astype(jnp.int32)
    return doc

def split3(v):
    a=v.astype(bf16).astype(f32); r=v-a
    b=r.astype(bf16).astype(f32); c=r-b
    return a,b,c

def augment(base, lane, head_lo, cols):
    keep=(lane<64) if head_lo else (lane>=64)
    off=64 if head_lo else 0
    out=jnp.where(keep, base, 0.0)
    for i,c in enumerate(cols):
        out=jnp.where(lane==off+i, c, out)
    return out.astype(bf16)

def onehot_part(base, lane, head_lo, doc, minus, scale):
    keep=(lane<64) if head_lo else (lane>=64)
    off=64 if head_lo else 0
    l=lane-off
    oh=jnp.where((l>=0)&(l<8), (jnp.where(l==doc,1.0,0.0)-minus)*scale, 0.0)
    return jnp.where(keep, base, oh)

def attn_fwd_pair(p, q_ref,k_ref,v_ref, ctx_ref, lse_ref, doc):
    cols=pl.ds(pl.multiple_of(p*128,128),128)
    lane=lax.broadcasted_iota(jnp.int32,(PACK,128),1)
    kp=k_ref[:,cols].astype(f32)
    vp=v_ref[:,cols]
    kk=[onehot_part(kp,lane,lo,doc,1.0,1.0).astype(bf16) for lo in (True,False)]
    laneb=lax.broadcasted_iota(jnp.int32,(QB,128),1)
    for b in range(PACK//QB):
        rows=pl.ds(b*QB,QB)
        qp=q_ref[rows,cols].astype(f32)*0.125
        docb=doc[b*QB:(b+1)*QB]
        outs=[]
        lse_old=lse_ref[rows,:]
        for h,lo in enumerate((True,False)):
            qa=onehot_part(qp,laneb,lo,docb,0.0,BIG).astype(bf16)
            s=dot(qa,kk[h],1,1)
            m=jnp.max(s,axis=1,keepdims=True)
            e=jnp.exp(s-m)
            l=jnp.sum(e,axis=1,keepdims=True)
            o=dot(e.astype(bf16),vp)
            outs.append(o/l)
            lse_old=jnp.where(laneb==2*p+h, m+jnp.log(l), lse_old)
        lse_ref[rows,:]=lse_old
        ctx_ref[rows,cols]=jnp.where(laneb<64,outs[0],outs[1]).astype(bf16)

def layer_norm(z):
    mu=jnp.mean(z,axis=-1,keepdims=True)
    c=z-mu
    r=lax.rsqrt(jnp.mean(c*c,axis=-1,keepdims=True)+NORM_EPS)
    return c*r, r

def ka_body(len_ref,x_ref,wa_ref,p_ref,q_ref,k_ref,v_ref,ctx_ref,lse_ref,hid_ref,r1_ref,w_ref):
    pltpu.sync_copy(wa_ref.at[pl.ds(0,4)],w_ref)
    doc=doc_column(len_ref,(PACK,1),0)
    for i,(o,b) in enumerate(((q_ref,0),(k_ref,None),(v_ref,1))):
        for t in range(4):
            rows=pl.ds(t*256,256)
            y=dot(x_ref[rows,:],w_ref[i])
            if b is not None: y=y+p_ref[b:b+1,:]
            o[rows,:]=y.astype(bf16)
    def body(p,c):
        attn_fwd_pair(p,q_ref,k_ref,v_ref,ctx_ref,lse_ref,doc)
        return c
    lax.fori_loop(0,6,body,0)
    for t in range(4):
        rows=pl.ds(t*256,256)
        z=x_ref[rows,:].astype(f32)+(dot(ctx_ref[rows,:],w_ref[3])+p_ref[2:3,:])
        n,r=layer_norm(z)
        hid_ref[rows,:]=n
        r1_ref[rows,:]=jnp.broadcast_to(r,(256,128))

def call_a(lengths,x,w,params):
    V=pltpu.VMEM
    return pl.pallas_call(ka_body,
        in_specs=[pl.BlockSpec(memory_space=pltpu.SMEM),pl.BlockSpec(memory_space=V),pl.BlockSpec(memory_space=pl.ANY),pl.BlockSpec(memory_space=V)],
        out_specs=[pl.BlockSpec(memory_space=V)]*7,
        out_shape=[jax.ShapeDtypeStruct((PACK,D),bf16)]*4+[jax.ShapeDtypeStruct((PACK,128),f32),jax.ShapeDtypeStruct((PACK,D),f32),jax.ShapeDtypeStruct((PACK,128),f32)],
        scratch_shapes=[V((4,D,D),bf16)],
        compiler_params=pltpu.CompilerParams(vmem_limit_bytes=60<<20))(lengths,x,w,params)

def gelu_both(x):
    z=jnp.abs(x)*0.7071067811865476
    t=1.0/(1.0+0.3275911*z)
    e=jnp.exp(-0.5*x*x)
    poly=t*(0.254829592+t*(-0.284496736+t*(1.421413741+t*(-1.453152027+t*1.061405429))))
    half=0.5*poly*e
    phi_c=jnp.where(x>=0,1.0-half,half)
    return x*phi_c, phi_c+x*(e*0.3989422804014327)

def kb_body(cot_ref,n1_ref,r1_ref,ctx_ref,w_ref,p_ref, out_ref,dz1_ref,dctx_ref,dwo_ref,dw1_ref,dw2_ref,vec_ref, act_ref,gp_ref,dffn_ref,hlow_ref):
    TT=256
    g1,s1,g2,s2=(p_ref[i:i+1,:] for i in (8,9,10,11))
    b2=p_ref[7:8,:]
    vec_ref[...]=jnp.zeros_like(vec_ref)
    def tile(t,carry):
        rows=pl.ds(pl.multiple_of(t*TT,TT),TT)
        n1=n1_ref[rows,:]
        hid=n1*g1+s1
        hl=hid.astype(bf16)
        hlow_ref[rows,:]=hl
        ffn=None
        for c in range(4):
            inner=dot(hl,w_ref[4+c])+p_ref[3+c:4+c,:]
            a,gp=gelu_both(inner)
            al=a.astype(bf16)
            act_ref[rows,pl.ds(c*D,D)]=al
            gp_ref[rows,pl.ds(c*D,D)]=gp.astype(gp_ref.dtype)
            y=dot(al,w_ref[8+c])
            ffn=y if ffn is None else ffn+y
        z=hid+(ffn+b2)
        n2,r2=layer_norm(z)
        out_ref[rows,:]=(n2*g2+s2).astype(bf16)
        e=cot_ref[rows,:].astype(f32)
        c2=e*g2
        dz2=r2*(c2-jnp.mean(c2,axis=-1,keepdims=True)-n2*jnp.mean(c2*n2,axis=-1,keepdims=True))
        dffn=dz2.astype(bf16)
        dffn_ref[rows,:]=dffn
        vec_ref[10:11,:]+=jnp.sum(e*n2,axis=0,keepdims=True)
        vec_ref[11:12,:]+=jnp.sum(e,axis=0,keepdims=True)
        vec_ref[7:8,:]+=jnp.sum(dffn.astype(f32),axis=0,keepdims=True)
        dh=dz2
        for c in range(4):
            dact=dot(dffn,w_ref[8+c],1,1)
            din=(dact*gp_ref[rows,pl.ds(c*D,D)].astype(f32)).astype(bf16)
            gp_ref[rows,pl.ds(c*D,D)]=din.astype(gp_ref.dtype)
            vec_ref[3+c:4+c,:]+=jnp.sum(din.astype(f32),axis=0,keepdims=True)
            dh=dh+dot(din,w_ref[4+c],1,1)
        vec_ref[8:9,:]+=jnp.sum(dh*n1,axis=0,keepdims=True)
        vec_ref[9:10,:]+=jnp.sum(dh,axis=0,keepdims=True)
        c1=dh*g1
        dz1=r1_ref[rows,0:1]*(c1-jnp.mean(c1,axis=-1,keepdims=True)-n1*jnp.mean(c1*n1,axis=-1,keepdims=True))
        dz1_ref[rows,:]=dz1
        dat=dz1.astype(bf16)
        vec_ref[2:3,:]+=jnp.sum(dat.astype(f32),axis=0,keepdims=True)
        dctx_ref[rows,:]=dot(dat,w_ref[3],1,1).astype(bf16)
        return carry
    lax.fori_loop(0,PACK//TT,tile,0)
    for c in range(4):
        dw2_ref[c]=dot(act_ref[:,c*D:(c+1)*D],dffn_ref[...],0,0).astype(bf16)
        dw1_ref[c]=dot(hlow_ref[...],gp_ref[:,c*D:(c+1)*D].astype(bf16),0,0).astype(bf16)
    dwo_ref[...]=dot(ctx_ref[...],dz1_ref[...].astype(bf16),0,0).astype(bf16)

def call_b(cot,n1,r1,ctx,w,params):
    V=pltpu.VMEM
    S=jax.ShapeDtypeStruct
    return pl.pallas_call(kb_body,
        in_specs=[pl.BlockSpec(memory_space=V)]*6,
        out_specs=[pl.BlockSpec(memory_space=V)]*7,
        out_shape=[S((PACK,D),bf16),S((PACK,D),f32),S((PACK,D),bf16),S((D,D),bf16),S((4,D,D),bf16),S((4,D,D),bf16),S((16,D),f32)],
        scratch_shapes=[V((PACK,FF),bf16),V((PACK,FF),bf16),V((PACK,D),bf16),V((PACK,D),bf16)],
        compiler_params=pltpu.CompilerParams(vmem_limit_bytes=62<<20))(cot,n1,r1,ctx,w,params)

def kc_body(len_ref,x_ref,q_ref,k_ref,v_ref,ctx_ref,do_ref,lse_ref,dz1_ref,wa_ref, ig_ref,dw_ref,vec_ref, dqkv_ref, dqa_ref,w_ref):
    pltpu.sync_copy(wa_ref.at[pl.ds(0,3)],w_ref)
    doc=doc_column(len_ref,(PACK,1),0)
    lane=lax.broadcasted_iota(jnp.int32,(PACK,128),1)
    KB_=256
    def pair(p,carry):
        cols=pl.ds(pl.multiple_of(p*128,128),128)
        qp=q_ref[:,cols].astype(f32); kp=k_ref[:,cols].astype(f32); vp=v_ref[:,cols].astype(f32)
        dop=do_ref[:,cols].astype(f32); cp=ctx_ref[:,cols].astype(f32)
        prod=dop*cp
        qa=[];qm=[];doa=[];dom=[];ka=[];km=[];va=[]
        for h,lo in enumerate((True,False)):
            keep=(lane<64) if lo else (lane>=64)
            off=64 if lo else 0
            lse=jnp.sum(jnp.where(lane==2*p+h,lse_ref[...],0.0),axis=1,keepdims=True)
            dd=jnp.sum(jnp.where(keep,prod,0.0),axis=1,keepdims=True)
            q1=onehot_part(qp*0.125,lane,lo,doc,0.0,BIG)
            for i,c in enumerate(split3(-lse)): q1=jnp.where(lane==off+8+i,c,q1)
            qa.append(q1.astype(bf16)); qm.append(jnp.where(keep,qp*0.125,0.0).astype(bf16))
            k1=onehot_part(kp,lane,lo,doc,1.0,1.0)
            k1=jnp.where((lane>=off+8)&(lane<off+11),1.0,k1)
            ka.append(k1.astype(bf16)); km.append(jnp.where(keep,kp*0.125,0.0).astype(bf16))
            d1=jnp.where(keep,dop,0.0)
            dom.append(d1.astype(bf16))
            for i,c in enumerate(split3(-dd)): d1=jnp.where(lane==off+i,c,d1)
            doa.append(d1.astype(bf16))
            v1=jnp.where(keep,vp,0.0); v1=jnp.where((lane>=off)&(lane<off+3),1.0,v1)
            va.append(v1.astype(bf16))
        for b in range(PACK//KB_):
            rows=slice(b*KB_,(b+1)*KB_)
            dv=None;dk=None;dq=None
            for h in range(2):
                s=dot(ka[h][rows],qa[h],1,1)
                pr=jnp.exp(s)
                dp=dot(va[h][rows],doa[h],1,1)
                ds=(pr*dp).astype(bf16)
                a=dot(pr.astype(bf16),dom[h]); dv=a if dv is None else dv+a
                a=dot(ds,qm[h]); dk=a if dk is None else dk+a
                a=dot(ds,km[h][rows],0,0); dq=a if dq is None else dq+a
            if b==0: dqa_ref[...]=dq
            else: dqa_ref[...]+=dq
            dqkv_ref[1,rows,cols]=dk.astype(bf16)
            dqkv_ref[2,rows,cols]=dv.astype(bf16)
        dqkv_ref[0,:,cols]=dqa_ref[...].astype(bf16)
        for i in range(3):
            d=dqkv_ref[i,:,cols]
            dw_ref[i,:,cols]=dot(x_ref[...],d,0,0).astype(bf16)
            vec_ref[i:i+1,cols]=jnp.sum(d.astype(f32),axis=0,keepdims=True)
        return carry
    lax.fori_loop(0,6,pair,0)
    for t in range(4):
        rows=pl.ds(t*256,256)
        acc=dz1_ref[rows,:]
        for i in range(3):
            acc=acc+dot(dqkv_ref[i,rows,:],w_ref[i],1,1)
        ig_ref[rows,:]=acc

def call_c(lengths,x,q,k,v,ctx,do,lse,dz1,w):
    V=pltpu.VMEM; S=jax.ShapeDtypeStruct
    return pl.pallas_call(kc_body,
        in_specs=[pl.BlockSpec(memory_space=pltpu.SMEM)]+[pl.BlockSpec(memory_space=V)]*8+[pl.BlockSpec(memory_space=pl.ANY)],
        out_specs=[pl.BlockSpec(memory_space=V)]*3,
        out_shape=[S((PACK,D),f32),S((3,D,D),bf16),S((8,D),f32)],
        scratch_shapes=[V((3,PACK,D),bf16),V((PACK,128),f32),V((3,D,D),bf16)],
        compiler_params=pltpu.CompilerParams(vmem_limit_bytes=62<<20))(lengths,x,q,k,v,ctx,do,lse,dz1,w)

RB=256
def diag_sum(blk):
    i=lax.broadcasted_iota(jnp.int32,blk.shape,0); j=lax.broadcasted_iota(jnp.int32,blk.shape,1)
    return jnp.sum(jnp.where(i==j,blk,0.0),keepdims=True)
def eye_rows(rb):
    i=lax.broadcasted_iota(jnp.int32,(RB,D),0)+rb*RB; j=lax.broadcasted_iota(jnp.int32,(RB,D),1)
    return i==j
def newton(m_ref,x_ref,nb_ref,pb_ref,sb_ref,xb_ref):
    nblk=D//RB
    R=[slice(i*RB,(i+1)*RB) for i in range(nblk)]
    tot=jnp.zeros((1,1),f32); tr=jnp.zeros((1,1),f32)
    for i in range(nblk):
        blk=m_ref[R[i],:]
        tot=tot+jnp.sum(blk*blk,keepdims=True)
        tr=tr+diag_sum(blk[:,R[i]])
    c=jnp.sqrt(tot+1e-6)
    inv=1.0/c
    al=tr*inv/D
    s=lax.rsqrt(jnp.sqrt(c))
    for i in range(nblk):
        m_ref[R[i],:]=m_ref[R[i],:]*inv
    def iteration(k,al,be,first=False,last=False):
        u=5-al
        u2=u*u;u3=u2*u;u4=u2*u2
        c0=al*u4*(1/256); c1=(u4-4*al*u3)*(1/256); c2=(12*al*u2-8*u3)*(1/512)
        c3=(36*u2-24*al*u)*(1/1536); c4=(24*al-96*u)*(1/6144); c5=1/256
        for i in range(nblk):
            nb_ref[R[i],:]=jnp.where(eye_rows(i),m_ref[R[i],:]-al,m_ref[R[i],:]).astype(bf16)
            if not first: xb_ref[R[i],:]=jnp.where(eye_rows(i),x_ref[R[i],:]-be,x_ref[R[i],:]).astype(bf16)
        be2=jnp.zeros((1,1),f32); al2=jnp.zeros((1,1),f32)
        for i in range(nblk):
            n=jnp.where(eye_rows(i),m_ref[R[i],:]-al,m_ref[R[i],:])
            if not last:
                p=dot(nb_ref[R[i],:],nb_ref[...])
                pb_ref[R[i],:]=p.astype(bf16)
                m=c1*n+c2*p
                m_ref[R[i],:]=jnp.where(eye_rows(i),m+c0,m)
            if first:
                x=jnp.where(eye_rows(i),1.25-al*0.25,0.0)-0.25*n
            else:
                x=(1.25-al*0.25)*x_ref[R[i],:]-0.25*(be*n+dot(xb_ref[R[i],:],nb_ref[...]))
            x_ref[R[i],:]=x
            be2=be2+diag_sum(x[:,R[i]])
        if not last:
            for i in range(nblk):
                q=dot(nb_ref[R[i],:],pb_ref[...])
                sb_ref[R[i],:]=(c3*nb_ref[R[i],:].astype(f32)+c4*pb_ref[R[i],:].astype(f32)+c5*q).astype(bf16)
            for i in range(nblk):
                m=m_ref[R[i],:]+dot(pb_ref[R[i],:],sb_ref[...])
                m_ref[R[i],:]=m
                al2=al2+diag_sum(m[:,R[i]])
        return al2*(1/D),be2*(1/D)
    al,be=iteration(0,al,None,first=True)
    al,be=lax.fori_loop(1,7,lambda k,ab:iteration(k,*ab),(al,be))
    iteration(7,al,be,last=True)
    for i in range(nblk):
        x_ref[R[i],:]=x_ref[R[i],:]*s
def body(a_ref,x_ref,m_ref,nb,pb,sb,xb):
    m_ref[...]=a_ref[...]
    newton(m_ref,x_ref,nb,pb,sb,xb)
def call_newton(a):
    V=pltpu.VMEM
    return pl.pallas_call(body,in_specs=[pl.BlockSpec(memory_space=V)],out_specs=pl.BlockSpec(memory_space=V),
      out_shape=jax.ShapeDtypeStruct((D,D),f32),scratch_shapes=[V((D,D),f32)]+[V((D,D),bf16)]*4,
      compiler_params=pltpu.CompilerParams(vmem_limit_bytes=60<<20))(a)

NZ=4; MR=48; HC=384
MESH=pl.DeviceIdType.MESH
def rcopy(src,dst,ss,rs,dev):
    return pltpu.make_async_remote_copy(src_ref=src,dst_ref=dst,send_sem=ss,recv_sem=rs,device_id=dev,device_id_type=MESH)

class Place:
    def __init__(self):
        self.dp=lax.axis_index("dp"); self.head=lax.axis_index("head")
        self.z=self.dp//2; self.x=self.dp%2; self.y=self.head//2; self.c=self.head%2
        self.xy=self.x*2+self.y
        self.chip=self.z*4+self.xy
        self.me=self.dp*4+self.head
        self.xn=((self.dp//2)*2+(1-self.x), self.head)
        self.yn=(self.dp,(1-self.y)*2+self.c)
        self.sib=(self.dp,self.y*2+(1-self.c))
        self.cols=pl.ds(pl.multiple_of(self.c*HC,128),HC)
        self.ocols=pl.ds(pl.multiple_of((1-self.c)*HC,128),HC)
    def zpeer(self,k):
        return (((self.z+k)%NZ)*2+self.x,self.head)
    def zfrom(self,k):
        return (self.z+NZ-k)%NZ
    def neighbours(self):
        return [self.zpeer(1),self.zpeer(2),self.zpeer(3),self.xn,self.yn,self.sib]

def greet(devs):
    bar=pltpu.get_barrier_semaphore()
    for d in devs:
        pl.semaphore_signal(bar,inc=1,device_id=d,device_id_type=MESH)
    pl.semaphore_wait(bar,len(devs))

def greet_all(pc):
    bar=pltpu.get_barrier_semaphore()
    def sig(k,carry):
        t=(pc.me+k)%32
        pl.semaphore_signal(bar,inc=1,device_id=(t//4,t%4),device_id_type=MESH)
        return carry
    lax.fori_loop(1,32,sig,0)
    pl.semaphore_wait(bar,31)

class Gather:
    def __init__(self,pc,buf,ss,rs):
        self.pc,self.buf,self.ss,self.rs=pc,buf,ss,rs
    def region(self,z,xy,mine=True):
        pc=self.pc
        return self.buf.at[z,xy,:,pc.cols if mine else pc.ocols]
    def copies(self):
        pc=self.pc; al=pl.ds(0,4); lo=pl.ds(0,2); hi=pl.ds(2,2)
        xo=(1-pc.x)*2+pc.y; yo=pc.x*2+(1-pc.y); dg=(1-pc.x)*2+(1-pc.y)
        R=self.region
        def mk(i,src,dst,dev):
            return rcopy(src,dst,self.ss.at[i],self.rs.at[i],dev)
        send={}
        for k in (1,2,3): send[k-1]=(R(pc.z,pc.xy),pc.zpeer(k))
        send[3]=(R(al,pc.xy),pc.xn); send[4]=(R(al,pc.xy),pc.yn)
        send[5]=(R(hi,yo),pc.xn); send[6]=(R(lo,xo),pc.yn)
        send[7]=(R(al,pc.xy),pc.sib); send[8]=(R(al,xo),pc.sib); send[9]=(R(al,yo),pc.sib); send[10]=(R(al,dg),pc.sib)
        recv={}
        for k in (1,2,3): recv[k-1]=R(pc.zfrom(k),pc.xy)
        recv[3]=R(al,xo); recv[4]=R(al,yo); recv[5]=R(hi,dg); recv[6]=R(lo,dg)
        recv[7]=R(al,pc.xy,False); recv[8]=R(al,xo,False); recv[9]=R(al,yo,False); recv[10]=R(al,dg,False)
        self.send=[mk(i,send[i][0],send[i][0],send[i][1]) for i in range(11)]
        self.recv=[mk(i,recv[i],recv[i],pc.sib) for i in range(11)]
        return self
    def step0(self):
        for i in (0,1,2): self.send[i].start()
    def step1(self):
        for i in (0,1,2): self.recv[i].wait_recv()
        for i in (3,4,7): self.send[i].start()
    def step2(self):
        self.recv[3].wait_recv()
        for i in (6,8): self.send[i].start()
        self.recv[4].wait_recv()
        for i in (5,9): self.send[i].start()
    def step3(self):
        for i in (5,6): self.recv[i].wait_recv()
        self.send[10].start()
    def step4(self):
        for i in (7,8,9,10): self.recv[i].wait_recv()
    def done(self):
        for i in range(11): self.send[i].wait_send()
    def step(self,i):
        (self.step0,self.step1,self.step2,self.step3,self.step4)[i]()

ORDER=(0,1,2,3,4,8,5,9,6,10,7,11)
def ag_body(mas_ref,pv_ref,left_ref,right_ref, w_ref,pg_ref,st_ref, sibm,ss,rs,cs,cr,ts,tr,lsem):
    pc=Place()
    greet_all(pc)
    half=rcopy(mas_ref.at[:,:,pc.ocols],sibm,cs,cr,pc.sib)
    half.start()
    def stat(b,act):
        t=(b%4)*4+b//4
        for side,ref in enumerate((left_ref,right_ref)):
            dev=((t//2),(t%2)*2+side)
            idx=b*2+side
            mine=(pc.chip==t)&(pc.c==side)
            act(idx,ref.at[b],dev,mine)
    half.wait_recv()
    lo=pl.ds(0,24); hi=pl.ds(24,24)
    for b in ORDER:
        own=mas_ref[b,:,pc.cols]; oth=sibm[b]
        first=jnp.where(pc.c==0,own,oth); second=jnp.where(pc.c==0,oth,own)
        w_ref[b,pc.z,pc.xy,:,pc.cols]=jnp.concatenate([first,second],axis=0).astype(bf16)
    pg_ref[pc.z,pc.xy,:,pc.cols]=pv_ref[...]
    half.wait_send()
    gs=[Gather(pc,pg_ref,ss.at[12],rs.at[12]).copies()]+[Gather(pc,w_ref.at[b],ss.at[b],rs.at[b]).copies() for b in ORDER]
    for t in range(len(gs)+4):
        for s in range(5):
            if 0<=t-s<len(gs): gs[t-s].step(s)
    def start(b,carry):
        def act(idx,src,dev,mine):
            @pl.when(mine)
            def _(): pltpu.make_async_copy(src,st_ref.at[pc.me],tr).start()
            @pl.when(jnp.logical_not(mine))
            def _(): rcopy(src,st_ref.at[pc.me],ts.at[idx],tr,dev).start()
        stat(b,act)
        return carry
    lax.fori_loop(0,NB,start,0)
    for g in gs: g.done()
    def fin(b,carry):
        def act(idx,src,dev,mine):
            @pl.when(jnp.logical_not(mine))
            def _(): rcopy(src,st_ref.at[pc.me],ts.at[idx],tr,dev).wait_send()
        stat(b,act)
        return carry
    lax.fori_loop(0,NB,fin,0)
    @pl.when(pc.xy<3)
    def _(): pltpu.make_async_copy(st_ref,st_ref,tr).wait()

def call_ag(masters,pv,left,right):
    V=pltpu.VMEM; S=jax.ShapeDtypeStruct; A=pl.ANY
    B=lambda m: pl.BlockSpec(memory_space=m)
    sem=pltpu.SemaphoreType.DMA
    return pl.pallas_call(ag_body,in_specs=[B(V),B(V),B(A),B(A)],out_specs=[B(V),B(V),B(A)],
        out_shape=[S((NB,4,4,MR,D),bf16),S((4,4,16,D),bf16),S((32,24,D),f32)],
        scratch_shapes=[V((NB,24,HC),f32),sem((13,11)),sem((13,11)),sem,sem,sem((24,)),sem,sem],
        compiler_params=pltpu.CompilerParams(vmem_limit_bytes=60<<20,collective_id=0,has_side_effects=True))(masters,pv,left,right)

def params_of(pg):
    t=pg.reshape(16,16,2,HC)[:,:12,:,:24]
    return jnp.transpose(t,(1,0,2,3)).reshape(12,D).astype(f32)


class Scatter:
    def __init__(self,pc,b,g_ref,R,out_ref,gown_ref,ss,rs,os_,orr):
        self.pc,self.b,self.g=pc,b,g_ref.at[b]
        self.out,self.gown=out_ref,gown_ref
        self.os_,self.orr=os_,orr
        self.R={k:v.at[b] for k,v in R.items()}
        R=self.R
        s1,rc=R["s1"],R["rc"]
        def mk(i,src,dst,dev): return rcopy(src,dst,ss.at[b,i],rs.at[b,i],dev)
        lo=pl.ds(0,2); hi=pl.ds(2,2); al=pl.ds(0,4)
        self.core=mk(0,self.g.at[:,:,:,pc.ocols],rc,pc.sib)
        self.xa=mk(1,s1.at[lo,pl.ds((1-pc.x)*2,2)],R["xa"],pc.xn)
        self.yb=[mk(2+i,s1.at[hi,i*2+1-pc.y],R["yb"].at[i],pc.yn) for i in range(2)]
        self.ya=mk(4,R["s2a"],R["ya"],pc.yn)
        self.xb=mk(5,R["s2b"],R["xb"],pc.xn)
        self.zz=[mk(6+k-1,R["s3"].at[(pc.z+k)%NZ],R["zr"].at[k-1],pc.zpeer(k)) for k in (1,2,3)]
        self.home=mk(9,R["fin"].at[pl.ds(pl.multiple_of((1-pc.c)*24,8),24)],R["hr"],pc.sib)
        t=(b%4)*4+b//4
        self.t=t
        self.owner=[((t//2),(t%2)*2+side) for side in range(2)]
        self.to_owner=[rcopy(R["finb"],gown_ref.at[pc.chip,:,pc.cols],os_.at[b,side],orr,self.owner[side]) for side in range(2)]
        self.to_self=pltpu.make_async_copy(R["finb"],gown_ref.at[pc.chip,:,pc.cols],orr)
    def step0(self):
        self.core.start()
    def step1(self):
        pc=self.pc; R=self.R
        self.core.wait_recv()
        for z in range(4):
            R["s1"][z]=(self.g[z,:,:,pc.cols].astype(f32)+R["rc"][z].astype(f32)).astype(bf16)
        self.xa.start()
        for d in self.yb: d.start()
    def step2(self):
        pc=self.pc; R=self.R
        self.xa.wait_recv()
        s=R["s1"][0:2,pl.ds(pc.x*2,2)].astype(f32)+R["xa"][...].astype(f32)
        keep=jnp.where(pc.y==0,s[:,0],s[:,1]); give=jnp.where(pc.y==0,s[:,1],s[:,0])
        R["k2"][0:2]=keep; R["s2a"][...]=give.astype(bf16)
        self.ya.start()
        for d in self.yb: d.wait_recv()
        s0=R["s1"][2:4,pc.y].astype(f32)+R["yb"][0].astype(f32)
        s1=R["s1"][2:4,2+pc.y].astype(f32)+R["yb"][1].astype(f32)
        keep=jnp.where(pc.x==0,s0,s1); give=jnp.where(pc.x==0,s1,s0)
        R["k2"][2:4]=keep; R["s2b"][...]=give.astype(bf16)
        self.xb.start()
    def step3(self):
        R=self.R
        self.ya.wait_recv(); self.xb.wait_recv()
        a=R["k2"][0:2]+R["ya"][...].astype(f32)
        b=R["k2"][2:4]+R["xb"][...].astype(f32)
        R["k2"][0:2]=a; R["k2"][2:4]=b
        R["s3"][0:2]=a.astype(bf16); R["s3"][2:4]=b.astype(bf16)
        for d in self.zz: d.start()
    def step4(self):
        pc=self.pc; R=self.R
        for d in self.zz: d.wait_recv()
        s=R["k2"][pc.z]
        for k in range(3): s=s+R["zr"][k].astype(f32)
        R["fin"][...]=s
        R["finb"][...]=s.astype(bf16)
        self.home.start()
        @pl.when(pc.chip==self.t)
        def _():
            self.to_self.start()
            for side in range(2):
                @pl.when(pc.c!=side)
                def _(): self.to_owner[side].start()
        @pl.when(pc.chip!=self.t)
        def _():
            for d in self.to_owner: d.start()
    def step5(self):
        pc=self.pc; R=self.R
        self.home.wait_recv()
        own=R["fin"][pl.ds(pl.multiple_of(pc.c*24,8),24)]; oth=R["hr"][...]
        self.out[self.b,:,pc.cols]=own
        self.out[self.b,:,pc.ocols]=oth
    def step(self,i): (self.step0,self.step1,self.step2,self.step3,self.step4,self.step5)[i]()
    def done(self):
        pc=self.pc
        for d in [self.core,self.xa,*self.yb,self.ya,self.xb,*self.zz,self.home]: d.wait_send()
        @pl.when(pc.chip==self.t)
        def _():
            for side in range(2):
                @pl.when(pc.c!=side)
                def _(): self.to_owner[side].wait_send()
        @pl.when(pc.chip!=self.t)
        def _():
            for d in self.to_owner: d.wait_send()

def scatter_scratch(nb=NB):
    V=pltpu.VMEM
    return dict(s1=V((nb,4,4,MR,HC),bf16),rc=V((nb,4,4,MR,HC),bf16),xa=V((nb,2,2,MR,HC),bf16),yb=V((nb,2,2,MR,HC),bf16),
        s2a=V((nb,2,MR,HC),bf16),s2b=V((nb,2,MR,HC),bf16),ya=V((nb,2,MR,HC),bf16),xb=V((nb,2,MR,HC),bf16),
        k2=V((nb,4,MR,HC),f32),s3=V((nb,4,MR,HC),bf16),zr=V((nb,3,MR,HC),bf16),fin=V((nb,MR,HC),f32),finb=V((nb,MR,HC),bf16),hr=V((nb,24,HC),f32))

class VecSum:
    def __init__(self,pc,cur,buf,ss,rs):
        self.pc,self.cur,self.buf=pc,cur,buf
        zp=lambda bit: ((pc.z^bit)*2+pc.x,pc.head)
        z1=(pc.z+1-2*(pc.z%2)); z2=(pc.z+2)%4
        partners=[pc.sib,pc.xn,pc.yn,(z1*2+pc.x,pc.head),(z2*2+pc.x,pc.head)]
        self.d=[rcopy(cur.at[i],buf.at[i],ss.at[i],rs.at[i],p) for i,p in enumerate(partners)]
    def step(self,i):
        if i>0:
            self.d[i-1].wait_recv()
            self.cur[i]=self.cur[i-1]+self.buf[i-1]
        if i<5: self.d[i].start()
    def done(self):
        for d in self.d: d.wait_send()

RSORDER=(8,4,9,5,10,6,11,7,3,2,1,0)
KEYS=list(scatter_scratch())
def rs_body(g_ref,vec_ref,out_ref,vout_ref,gown_ref,*rest):
    R=dict(zip(KEYS,rest[:len(KEYS)])); vcur,vbuf,ss,rs,os_,orr,vs,vr=rest[len(KEYS):]
    pc=Place()
    greet_all(pc)
    vcur[0]=vec_ref[...]
    vsum=VecSum(pc,vcur,vbuf,vs,vr)
    sc=[Scatter(pc,b,g_ref,R,out_ref,gown_ref,ss,rs,os_,orr) for b in RSORDER]
    for t in range(len(sc)+5):
        for s in range(6):
            if 0<=t-s<len(sc): sc[t-s].step(s)
        if t<=5: vsum.step(t)
    vout_ref[...]=vcur[5]
    for s in sc: s.done()
    vsum.done()
    @pl.when(pc.xy<3)
    def _(): pltpu.make_async_copy(gown_ref,gown_ref,orr).wait()

def call_rs(g,vec):
    V=pltpu.VMEM; S=jax.ShapeDtypeStruct
    B=pl.BlockSpec(memory_space=V); sem=pltpu.SemaphoreType.DMA
    return pl.pallas_call(rs_body,in_specs=[B,B],out_specs=[B,B,B],
        out_shape=[S((NB,24,D),f32),S((16,D),f32),S((16,MR,D),bf16)],
        scratch_shapes=list(scatter_scratch().values())+[V((6,16,D),f32),V((5,16,D),f32),sem((NB,10)),sem((NB,10)),sem((NB,2)),sem,sem((5,)),sem((5,))],
        compiler_params=pltpu.CompilerParams(vmem_limit_bytes=62<<20,collective_id=1,has_side_effects=True))(g,vec)

BETA=0.95; BETA_TWO=0.99; RATE=1.0; RATE_VEC=0.05

def pack(rows):
    return jnp.concatenate([rows[:,:HC],rows[:,HC:]],axis=0).astype(bf16)
def unpack(p):
    p=p.astype(f32)
    return jnp.concatenate([p[:24],p[24:]],axis=1)

def send_rows(pc,n,base,slots,dst,ss,rsem,start):
    def one(j,carry):
        t=base+j
        @pl.when(t==pc.me)
        def _():
            if start: pltpu.make_async_copy(slots.at[j],dst,rsem).start()
        @pl.when(t!=pc.me)
        def _():
            d=rcopy(slots.at[j],dst,ss.at[j],rsem,(t//4,t%4))
            if start: d.start()
            else: d.wait_send()
        return carry
    lax.fori_loop(0,n,one,0)

def newton_body(gown_ref,stat_ref,left_ref,right_ref,mas_ref,va_ref,vec_ref,sec_ref,
                ln_ref,rn_ref,mn_ref,vg_ref,sn_ref,vn_ref,
                m_ref,x_ref,nb,pb,sb,xb,slots,ggr,uslots,ur,tb,rt,rho, gs,gr,us,ur_sem,es,er):
    pc=Place()
    greet_all(pc)
    b=pc.xy*4+pc.z
    owner=pc.xy<3
    nblk=D//RB
    @pl.when(owner)
    def _():
        for c in range(2):
            @pl.when(pc.c==c)
            def _():
                for i in range(nblk):
                    r=slice(i*RB,(i+1)*RB)
                    if c==0: p=dot(gown_ref[r,:],gown_ref[...],1,1)
                    else: p=dot(gown_ref[:,r],gown_ref[...],0,0)
                    x_ref[r,:]=(1-BETA)*p
                    m_ref[r,:]=BETA*stat_ref[r,:]+(1-BETA)*p
        def pk(i,carry):
            slots[i]=pack(x_ref[pl.ds(pl.multiple_of(i*24,8),24),:])
            return carry
        lax.fori_loop(0,32,pk,0)
        send_rows(pc,32,0,slots,ggr.at[2*b+pc.c],gs,gr,True)
        newton(m_ref,x_ref,nb,pb,sb,xb)
        tr=jnp.zeros((1,1),f32)
        for i in range(nblk):
            r=slice(i*RB,(i+1)*RB); tr=tr+diag_sum(x_ref[r,r])
        lam=tr*(1/D)
        for i in range(nblk):
            r=slice(i*RB,(i+1)*RB)
            xb[r,:]=jnp.where(eye_rows(i),x_ref[r,:]-lam,x_ref[r,:]).astype(bf16)
        H=D//2
        send_t=rcopy(tb.at[pl.ds(H,H)],tb.at[pl.ds(H,H)],es.at[0],er.at[0],pc.sib)
        send_r=rcopy(xb,rt,es.at[1],er.at[1],pc.sib)
        send_l=rcopy(rho.at[0],rho.at[1],es.at[2],er.at[2],pc.sib)
        def update(trows,right,lam_r):
            for i in range(2):
                r=pl.ds(trows+i*192,192)
                t=tb[r,:]
                m_ref[pl.ds(i*192,192),:]=lam_r*t.astype(f32)+dot(t,right[...])
        rho[0]=jnp.broadcast_to(lam,(8,128))
        @pl.when(pc.c==0)
        def _():
            for h in (1,0):
                for i in range(2):
                    r=slice(h*H+i*192,h*H+(i+1)*192)
                    tb[r,:]=(lam*gown_ref[r,:].astype(f32)+dot(xb[r,:],gown_ref[...])).astype(bf16)
                if h==1: send_t.start()
            send_r.wait_recv(); send_l.wait_recv()
            update(0,rt,rho[1,0:1,0:1])
            send_t.wait_send()
        @pl.when(pc.c==1)
        def _():
            send_r.start(); send_l.start()
            send_t.wait_recv()
            update(H,xb,lam)
            send_r.wait_send(); send_l.wait_send()
        def pk2(i,carry):
            uslots[i]=pack(m_ref[pl.ds(pl.multiple_of(i*24,8),24),:])
            return carry
        lax.fori_loop(0,16,pk2,0)
        send_rows(pc,16,pc.c*16,uslots,ur.at[b],us,ur_sem,True)
    r=lax.broadcasted_iota(jnp.int32,(D,128),1); j=lax.broadcasted_iota(jnp.int32,(D,128),0)
    pick=jnp.where((j==pc.me*24+r)&(r<24),1.0,0.0).astype(f32)
    vg=lax.dot_general(va_ref[...],pick,(((1,),(0,)),((),())),precision=lax.Precision.HIGHEST,preferred_element_type=f32)[:12,:24]
    sn=BETA_TWO*sec_ref[...]+(1-BETA_TWO)*vg*vg
    vg_ref[...]=vg; sn_ref[...]=sn
    vn_ref[...]=vec_ref[...]-RATE_VEC*vg/(jnp.sqrt(sn)+1e-8)
    pltpu.make_async_copy(ggr,ggr,gr).wait()
    def stats(i,carry):
        ln_ref[i]=BETA*left_ref[i]+unpack(ggr[2*i])
        rn_ref[i]=BETA*right_ref[i]+unpack(ggr[2*i+1])
        return carry
    lax.fori_loop(0,NB,stats,0)
    pltpu.make_async_copy(ur,ur,ur_sem).wait()
    def upd(i,carry):
        mn_ref[i]=mas_ref[i]-RATE*unpack(ur[i])
        return carry
    lax.fori_loop(0,NB,upd,0)
    @pl.when(owner)
    def _():
        send_rows(pc,32,0,slots,ggr.at[2*b+pc.c],gs,gr,False)
        send_rows(pc,16,pc.c*16,uslots,ur.at[b],us,ur_sem,False)

def call_newton_step(gown,stat,left,right,mas,va,vec,sec):
    V=pltpu.VMEM; S=jax.ShapeDtypeStruct
    B=pl.BlockSpec(memory_space=V); sem=pltpu.SemaphoreType.DMA
    rows=S((NB,24,D),f32); small=S((NB,24),f32)
    return pl.pallas_call(newton_body,in_specs=[B]*8,out_specs=[B]*6,out_shape=[rows]*3+[small]*3,
        scratch_shapes=[V((D,D),f32)]*2+[V((D,D),bf16)]*4+[V((32,48,HC),bf16),V((24,48,HC),bf16),V((16,48,HC),bf16),V((12,48,HC),bf16),V((D,D),bf16),V((D,D),bf16),V((2,8,128),f32),
            sem((32,)),sem,sem((16,)),sem,sem((3,)),sem((3,))],
        compiler_params=pltpu.CompilerParams(vmem_limit_bytes=62<<20,collective_id=2,has_side_effects=True))(gown,stat,left,right,mas,va,vec,sec)


def gather_rows(a):
    return lax.all_gather(a,("dp","head"),axis=1,tiled=True)

def doc_lengths(lengths):
    return lax.dynamic_slice_in_dim(lengths,lax.axis_index("head"),1,axis=0)

def layer(tokens,cotangent,lengths,w,params):
    q,k,v,ctx,lse,n1,r1=call_a(lengths,tokens,w,params)
    out,dz1,dctx,dwo,dw1,dw2,vec=call_b(cotangent,n1,r1,ctx,w,params)
    ig,dwqkv,vq=call_c(lengths,tokens,q,k,v,ctx,dctx,lse,dz1,w)
    terms=jnp.concatenate([dwqkv,dwo[None],dw1,dw2],axis=0)
    vec=jnp.concatenate([vq[0:1],vq[2:3],vec[2:]],axis=0)
    return out,ig,terms,vec

def on_slice(tokens,cotangent,lengths,masters,vectors,left,right,second):
    pv=jnp.pad(vectors,((0,4),(0,HC-24))).astype(bf16)
    w,pg,stat=call_ag(masters,pv,left,right)
    w=w.reshape(NB,D,D)
    params=params_of(pg)
    out,ig,terms,vec=layer(tokens,cotangent,doc_lengths(lengths),w,params)
    grads,vec_all,gown=call_rs(terms.reshape(NB,4,4,MR,D),vec)
    ln,rn,mn,vg,sn,vn=call_newton_step(gown.reshape(D,D),stat.reshape(D,D),left,right,masters,vec_all,vectors,second)
    return out,ig,grads,ln,rn,mn,vg,sn,vn

def on_any(tokens,cotangent,lengths,masters,vectors,left,right,second):
    axes=("dp","head")
    me=lax.axis_index("dp")*lax.axis_size("head")+lax.axis_index("head")
    share=masters.shape[1]
    w=gather_rows(masters.astype(bf16))
    params=gather_rows(vectors.astype(bf16)).astype(f32)
    out,ig,terms,vec=layer(tokens,cotangent,doc_lengths(lengths),w,params)
    grads=lax.psum_scatter(terms.astype(f32),axes,scatter_dimension=1,tiled=True)
    vg=lax.psum_scatter(vec[:12],axes,scatter_dimension=1,tiled=True)
    low=grads.astype(bf16)
    g=gather_rows(low)
    ein=partial(jnp.einsum,preferred_element_type=f32)
    cols=lax.dynamic_slice_in_dim(g,me*share,share,axis=2)
    ln=BETA*left+(1-BETA)*ein("kid,kjd->kij",low,g)
    rn=BETA*right+(1-BETA)*ein("kdi,kdj->kij",cols,g)
    item=jnp.minimum(me,2*NB-1)
    own=lax.dynamic_index_in_dim(jnp.concatenate([gather_rows(ln),gather_rows(rn)],axis=0),item,0,keepdims=False)
    root=call_newton(own)
    place=jnp.where((jnp.arange(2*NB)==me)[:,None,None],root[None],0.0)
    rows=lax.psum_scatter(place,axes,scatter_dimension=1,tiled=True)
    rr=gather_rows(rows[NB:])
    hi=partial(jnp.einsum,"kij,kjl->kil",precision=lax.Precision.HIGHEST)
    mn=masters-RATE*hi(hi(rows[:NB],g.astype(f32)),rr)
    sn=BETA_TWO*second+(1-BETA_TWO)*vg*vg
    vn=vectors-RATE_VEC*vg/(jnp.sqrt(sn)+1e-8)
    return out,ig,grads,ln,rn,mn,vg,sn,vn

def solution(mesh):
    rows=P(("dp","head"),None); blocks=P(None,("dp","head"),None); vecs=P(None,("dp","head"))
    on_device=on_slice if dict(mesh.shape)=={"dp":8,"head":4} else on_any
    return jax.shard_map(on_device,mesh=mesh,
        in_specs=(rows,rows,P("dp",None),blocks,vecs,blocks,blocks,vecs),
        out_specs=(rows,rows,blocks,blocks,blocks,blocks,vecs,vecs,vecs),check_vma=False)
```

time: 2210 us -> 503 us (0.23)
  waiting for transfers between devices: 1060 us -> 0 us
  matrix products: 552 us -> 0 us
  Pallas kernels: 0 us -> 468 us
  local copies, waits for them, and re-layouts: 290 us -> 11.3 us
  other arithmetic: 143 us -> 13.4 us
  blocking collectives: 104 us -> 0 us
  starting transfers between devices: 39.7 us -> 0 us
    dot_general x79 -> x0, matrix products: 552 us -> none  [the longest x38 342 us: batched(): return jnp.einsum('kij,kjl->kil', left, right, precision=PRECISE)]
    all_gather x11 -> x0, waiting for transfers between devices: 523 us -> none  [the longest x8 452 us: gather_iterate(): return lax.all_gather(matrix_rows, 'head', axis=1, tiled=True)]
    pallas_call x0 -> x6, Pallas kernels: none -> 468 us  [the longest x1 131 us: call_ag(): pl.pallas_call(ag_body, in_specs=[B(V), B(V), B(A), B(A)], out_specs=[B(V...]
    reduce_scatter x1 -> x0, waiting for transfers between devices: 347 us -> none  [on_device(): lax.psum_scatter(terms, ('dp', 'head'), scatter_dimension=1, tiled=True)]
    all_to_all x7 -> x0, waiting for transfers between devices: 185 us -> none  [the longest x1 52.7 us: on_device(): lax.all_to_all(projected, 'head', split_axis=1, concat_axis=0, tiled=True)]
    convert_element_type x7 -> x1, other arithmetic: 55.3 us -> 0.09 us  [params_of(): return jnp.transpose(t, (1, 0, 2, 3)).reshape(12, D).astype(f32)]
    unnamed x168 -> x27, local copies, waits for them, and re-layouts: 60.7 us -> 7.38 us
    unnamed x1 -> x0, blocking collectives: 40.1 us -> none
  transfers between devices with their start and end apart: 19 -> 0, of which waited for: 15 -> 0; matrix products, arithmetic and copies ran while one was open for 10% -> 0% of each run, Pallas kernels for 0% -> 0%
where the time goes in v1:
time: 503 us; the launch traced here: 494 us
  Pallas kernels  468 us (93%)
  other arithmetic  13.4 us (3%)
  local copies, waits for them, and re-layouts  11.3 us (2%)
    pallas_call x1, Pallas kernels, call_ag(): pl.pallas_call(ag_body, in_specs=[B(V), B(V), B(A), B(A)], out_specs=[B(V...  131 us
    pallas_call x1, Pallas kernels, call_rs(): pl.pallas_call(rs_body, in_specs=[B, B], out_specs=[B, B, B], out_shape=[...  112 us
    pallas_call x1, Pallas kernels, call_newton_step(): pl.pallas_call(newton_body, in_specs=[B] * 8, out_specs=[B] * 6, out_shap...  65.4 us
    pallas_call x1, Pallas kernels, call_c(): pl.pallas_call(kc_body, in_specs=[pl.BlockSpec(memory_space=pltpu.SMEM)]...  64.1 us
    pallas_call x1, Pallas kernels, call_b(): pl.pallas_call(kb_body, in_specs=[pl.BlockSpec(memory_space=V)] * 6, out_...  56.4 us
    pallas_call x1, Pallas kernels, call_a(): pl.pallas_call(ka_body, in_specs=[pl.BlockSpec(memory_space=pltpu.SMEM),...  39.1 us
    concatenate x1, other arithmetic, layer(): terms = jnp.concatenate([dwqkv, dwo[None], dw1, dw2], axis=0)  12 us

profile of v1, /device:TPU:11, one launch (start us, length us, event | category | flops | bytes accessed | tf_op | source)
XLA Modules:
  0.0 494.2 jit_solution(12135097915210480864)
XLA Ops:
  0.6 0.0 copy-start
  0.7 0.7 copy-done
  1.3 0.5 constant_dynamic-slice_fusion.len_ref
  1.8 0.7 convert.6
  2.5 0.6 pad.5.pv_ref
  3.2 130.9 %shard_map.151 = (bf16[12,4,4,48,768]{4,3,2,1,0:T(8,128)(2,1)}, bf16[4,4,16,768]{3,2,1,0:T(8,128)(2,1)}, f32[32,24,768]{2,1,0:T(8,128)}) custom-call(f32[12,24,768]{2,1,0:T(8,128)} %mas_ref.3, bf16[16,384]{1,0:T(8,128)(2,1)} %pad.5.pv_ref, f32[12,24,768]{2,1,0:T(8,128)} %left_ref.3, f32[12,24,768]{2,1,0:T(8,128)} %right_ref.3), custom_call_target="tpu_custom_call" | custom-call | tf_op jit(solution)/shard_map/pallas_call | solution.py:440
  134.0 1.1 reshape.40
  135.1 0.1 convert_bitcast_fusion
  135.2 0.9 reshape.43.p_ref
  136.1 39.1 %shard_map.152 = (bf16[1024,768]{1,0:T(8,128)(2,1)}, bf16[1024,768]{1,0:T(8,128)(2,1)}, bf16[1024,768]{1,0:T(8,128)(2,1)}, bf16[1024,768]{1,0:T(8,128)(2,1)}, f3...) custom-call(s32[1,8]{1,0:T(1,128)} %constant_dynamic-slice_fusion.len_ref, bf16[1024,768]{1,0:T(8,128)(2,1)} %x_ref.3, ...), custom_call_target="tpu_custom_call" | custom-call | tf_op jit(solution)/shard_map/pallas_call | solution.py:97
  175.2 56.4 %shard_map.153 = (bf16[1024,768]{1,0:T(8,128)(2,1)}, f32[1024,768]{1,0:T(8,128)}, bf16[1024,768]{1,0:T(8,128)(2,1)}, bf16[768,768]{1,0:T(8,128)(2,1)}, bf16[4,76...) custom-call(bf16[1024,768]{1,0:T(8,128)(2,1)} %cot_ref.1, ...), custom_call_target="tpu_custom_call" | custom-call | tf_op jit(solution)/shard_map/pallas_call | solution.py:169
  231.6 64.1 %shard_map.154 = (f32[1024,768]{1,0:T(8,128)}, bf16[3,768,768]{2,1,0:T(8,128)(2,1)}, f32[8,768]{1,0:T(8,128)}) custom-call(s32[1,8]{1,0:T(1,128)} %constant_dynamic-slice_fusion.len_ref, bf16[1024,768]{1,0:T(8,128)(2,1)} %x_ref.3, bf16[1024,768]{1,0:T(8,128)(2,1)} %get-tuple-element.44.q_ref, bf16[1024,768]{1,0:T(8,128)(2,1)} %get-tuple-element.45.k_ref, ...), custom_call_target="tpu_custom_call" | custom-call | tf_op jit(solution)/shard_map/pallas_call | solution.py:235
  295.7 12.0 %pad_maximum_fusion.g_ref = bf16[12,4,4,48,768]{4,3,2,1,0:T(8,128)(2,1)} fusion(bf16[4,4,4,48,768]{4,3,2,1,0:T(8,128)(2,1)} %bitcast.15, bf16[4,4,4,48,768]{4,3,2,1,0:T(8,128)(2,1)} %bitcast.14, bf16[1,4,4,48,768]{4,3,2,1,0:T(8,128)(2,1)S(1)} %bitcast.18, bf16[3,4,4,48,768]{4,3,2,1,0:T(8,128)(2,1)} %bitcast.16), kind=kLoop, calls=%fused_computation | loop fusion | flops 21233664 | bytes 28311552 | tf_op jit(solution)/shard_map/concatenate | solution.py:713
  307.7 0.8 fusion
  308.6 0.6 pad_maximum_fusion.1.vec_ref
  309.2 112.4 %shard_map.155 = (f32[12,24,768]{2,1,0:T(8,128)}, f32[16,768]{1,0:T(8,128)}, bf16[16,48,768]{2,1,0:T(8,128)(2,1)}) custom-call(bf16[12,4,4,48,768]{4,3,2,1,0:T(8,128)(2,1)} %pad_maximum_fusion.g_ref, f32[16,768]{1,0:T(8,128)} %pad_maximum_fusion.1.vec_ref), custom_call_target="tpu_custom_call" | custom-call | tf_op jit(solution)/shard_map/pallas_call | solution.py:581
  421.6 65.4 %shard_map.156 = (f32[12,24,768]{2,1,0:T(8,128)}, f32[12,24,768]{2,1,0:T(8,128)}, f32[12,24,768]{2,1,0:T(8,128)}, f32[12,24]{1,0:T(8,128)}, f32[12,24]{1,0:T(8,128)}, /*index=5*/f32[12,24]{1,0:T(8,128)}) custom-call(bf16[768,768]{1,0:T(8,128)(2,1)} %bitcast.19, f32[768,768]{1,0:T(8,128)} %bitcast.17, f32[12,24,768]{2,1,0:T(8,128)} %left_ref.3, ...), custom_call_target="tpu_custom_call" | custom-call | tf_op jit(solution)/shard_map/pallas_call | solution.py:697
  487.1 0.9 copy.27
  488.0 2.1 copy.28
  490.1 0.9 copy.29
  491.1 0.9 copy.30
  492.0 0.6 copy.31
  492.6 0.6 copy.32
  493.2 0.6 copy.33
  (19 shorter events, 0.0 us)
Async XLA Ops:
  0.6 0.7 copy-start
  231.6 64.1 %copy-start.2 = (bf16[768,768]{1,0:T(8,128)(2,1)S(1)}, bf16[768,768]{1,0:T(8,128)(2,1)}, u32[]{:S(2)}) copy-start(bf16[768,768]{1,0:T(8,128)(2,1)} %get-tuple-element.52) | copy-start | bytes 3538948
  295.7 12.8 %copy-start.6 = (f32[16,768]{1,0:T(8,128)S(1)}, f32[16,768]{1,0:T(8,128)}, u32[]{:S(2)}) copy-start(f32[16,768]{1,0:T(8,128)} %get-tuple-element.56) | copy-start | bytes 147460
  421.6 65.4 %copy-start.3 = (f32[12,24,768]{2,1,0:T(8,128)S(1)}, f32[12,24,768]{2,1,0:T(8,128)}, u32[]{:S(2)}) copy-start(f32[12,24,768]{2,1,0:T(8,128)} %get-tuple-element.80) | copy-start | bytes 2654212
  487.0 3.1 copy-start.5
  487.0 4.0 copy-start.4
  487.0 6.7 %copy-start.1 = (s32[4,8]{1,0:T(4,128)S(1)}, s32[4,8]{1,0:T(4,128)}, u32[]{:S(2)}) copy-start(s32[4,8]{1,0:T(4,128)} %param.10) | copy-start | bytes 388
  487.1 4.9 copy-start.9
  487.1 5.5 %copy-start.8 = (f32[12,24]{1,0:T(8,128)S(1)}, f32[12,24]{1,0:T(8,128)}, u32[]{:S(2)}) copy-start(f32[12,24]{1,0:T(8,128)} %get-tuple-element.85) | copy-start | bytes 3460
  487.1 6.1 %copy-start.7 = (f32[12,24]{1,0:T(8,128)S(1)}, f32[12,24]{1,0:T(8,128)}, u32[]{:S(2)}) copy-start(f32[12,24]{1,0:T(8,128)} %get-tuple-element.86) | copy-start | bytes 3460
